TPU v7x, 512 devices: a whole 4x4x16 slice. The times are simulated.
512 devices in a mesh: ctx: 64 (over y, z), exp: 8 (over x, core).
Axes of the slice: x: 4, y: 4, z: 16, core: 2. Of those that a mesh axis runs over, the one named last changes fastest.
Arguments:
- x_resid: bfloat16 [512, 6144], P('exp', 'ctx'), may hold values from -16 to 16
- queries: bfloat16 [512, 6144], P('ctx', 'exp'), may hold values from -5 to 5
- keys: bfloat16 [32768, 1024], P('ctx', 'exp'), may hold values from -4 to 4
- values: bfloat16 [32768, 1024], P('ctx', 'exp'), may hold values from -4 to 4
- pattern: int32 [4, 6], replicated, may hold values from 0 to 254, as said below
- global_blocks: int32 [2], replicated, may hold values from 0 to 248, as said below
- out_weight: bfloat16 [6144, 6144], P('exp', 'ctx'), may hold values from -0.875 to 0.875
- norm_gain: float32 [6144], P('ctx'), may hold values from 0.1 to 1.9
- router: bfloat16 [6144, 8], P('ctx'), may hold values from -0.078125 to 0.078125
- expert_ids: int32 [512, 2], P('exp'), may hold values from 0 to 7, as said below
- expert_slots: int32 [512, 2], P('exp'), may hold values from 0 to 19, as said below
- w_gate: bfloat16 [8, 6144, 8192], P('exp', None, 'ctx'), may hold values from -0.078125 to 0.078125
- w_up: bfloat16 [8, 6144, 8192], P('exp', None, 'ctx'), may hold values from -0.078125 to 0.078125
- w_down: bfloat16 [8, 8192, 6144], P('exp', None, 'ctx'), may hold values from -0.0625 to 0.0625
Outputs:
- layer_out: bfloat16 [512, 6144], P('exp', 'ctx')
Inputs may be any that keep to these rules, and one draw needn't show every extreme that they name: `pattern`: each row lists 3 + 3 different key blocks, none of them a global block. `global_blocks`: 2 different key blocks. `expert_ids`: each token names two different experts; among the tokens of one index of exp (aligned blocks of 64 rows) every expert is named at most 20 times, and one expert, the same in every block, exactly 20 times. `expert_slots`: within one aligned block of 64 rows, the choices that name the same expert have different slots.
All inputs are finite; a program needn't handle non-finite values.
Results may differ from a plain program's by a relative error of at most 0.01.
Values may be sent and summed in bfloat16 or wider, within the bound.
No kernel may reach another device: no remote copies, remote signals or barrier semaphores. Data moves between devices by JAX's collectives and lax.ppermute only.
A program may use at most 64 MiB of HBM per device.

v0:
```python
import jax
import jax.numpy as jnp
from jax import lax
from jax.sharding import PartitionSpec as P

D = 6144
HD = 128
BLK = 128
CAP = 20
eps = 1e-05
masked_score = -1e30


def per_device(
    x_resid,
    queries,
    keys,
    values,
    pattern,
    global_blocks,
    out_weight,
    norm_gain,
    router,
    expert_ids,
    expert_slots,
    w_gate,
    w_up,
    w_down,
):
    all_queries = lax.all_gather(queries, "ctx", axis=0, tiled=True)
    token_count = all_queries.shape[0]
    cache_length = keys.shape[0]
    groups_local = keys.shape[1] // HD
    group = all_queries.shape[1] // HD // groups_local
    query_heads = all_queries.reshape(token_count, groups_local, group, HD)
    key_heads = keys.reshape(cache_length, groups_local, HD)
    value_heads = values.reshape(cache_length, groups_local, HD)
    scores = jnp.einsum(
        "tkgd,pkd->tkgp", query_heads, key_heads, preferred_element_type=jnp.float32
    ) * HD ** (-0.5)
    local_blocks = cache_length // BLK
    block_ids = lax.axis_index("ctx") * local_blocks + jnp.arange(local_blocks, dtype=jnp.int32)
    listed = jnp.any(pattern[:, :, None] == block_ids[None, None, :], axis=1)
    anchored = jnp.any(global_blocks[:, None] == block_ids[None, :], axis=0)
    allowed_blocks = listed | anchored[None, :]
    allowed = jnp.repeat(jnp.repeat(allowed_blocks, BLK, axis=0), BLK, axis=1)[:, None, None, :]
    local_peak = jnp.max(jnp.where(allowed, scores, masked_score), axis=-1)
    peak = lax.pmax(local_peak, "ctx")
    probs = jnp.where(allowed, jnp.exp(scores - peak[..., None]), 0.0).astype(jnp.bfloat16)
    numerator = jnp.einsum("tkgp,pkd->tkgd", probs, value_heads, preferred_element_type=jnp.float32)
    denominator = jnp.sum(probs, axis=-1, dtype=jnp.float32)
    numerator, denominator = lax.psum((numerator, denominator), "ctx")
    attention = (numerator / denominator[..., None]).astype(jnp.bfloat16).reshape(token_count, -1)
    exp_count = lax.axis_size("exp")
    head_total = lax.psum_scatter(
        jnp.dot(attention, out_weight, preferred_element_type=jnp.float32),
        "exp",
        scatter_dimension=0,
        tiled=True,
    )
    residual = x_resid.astype(jnp.float32) + head_total
    scaled = residual * norm_gain
    router_wide = router.astype(jnp.float32)
    squares = lax.psum(jnp.sum(residual * residual, axis=1), "ctx")
    inverse = lax.rsqrt(squares / D + eps)
    logits = lax.psum(
        jnp.dot(scaled * inverse[:, None], router_wide, precision=lax.Precision.HIGHEST), "ctx"
    )
    normed = (scaled * inverse[:, None]).astype(jnp.bfloat16)
    experts_all = router.shape[1]
    onehot = expert_ids[:, :, None] == jnp.arange(experts_all, dtype=jnp.int32)[None, None, :]
    chosen_logits = jnp.sum(jnp.where(onehot, logits[:, None, :], 0.0), axis=-1)
    gate_weights = jax.nn.sigmoid(chosen_logits - chosen_logits[:, ::-1])
    flat_slots = expert_ids * CAP + expert_slots
    positions = jnp.arange(experts_all * CAP, dtype=jnp.int32)
    dispatch = jnp.sum(
        (flat_slots[None, :, :] == positions[:, None, None]).astype(jnp.bfloat16), axis=2
    )
    local_experts = w_gate.shape[0]
    feature_rows = lax.all_gather(normed, "ctx", axis=1, tiled=True)
    outgoing = jnp.dot(dispatch, feature_rows, preferred_element_type=jnp.float32).astype(
        jnp.bfloat16
    )
    outgoing = outgoing.reshape(experts_all, CAP, -1)
    incoming = lax.all_to_all(outgoing, "exp", split_axis=0, concat_axis=0, tiled=True)
    incoming = incoming.reshape(exp_count, local_experts, CAP, -1)
    expert_gate = jnp.einsum("sjcd,jdf->sjcf", incoming, w_gate, preferred_element_type=jnp.float32)
    expert_lift = jnp.einsum("sjcd,jdf->sjcf", incoming, w_up, preferred_element_type=jnp.float32)
    hidden = (jax.nn.silu(expert_gate) * expert_lift).astype(jnp.bfloat16)
    out_width = w_down.shape[2]
    expert_out = jnp.einsum(
        "sjcf,jfd->sjcd",
        lax.all_gather(hidden, "ctx", axis=3, tiled=True),
        w_down,
        preferred_element_type=jnp.float32,
    ).astype(jnp.bfloat16)
    returned = lax.all_to_all(
        expert_out.reshape(experts_all, CAP, out_width),
        "exp",
        split_axis=0,
        concat_axis=0,
        tiled=True,
    )
    picked = jnp.take(returned.reshape(experts_all * CAP, out_width), flat_slots, axis=0).astype(
        jnp.float32
    )
    mixture = jnp.sum(gate_weights[:, :, None] * picked, axis=1)
    return (residual + mixture).astype(jnp.bfloat16)


def solution(mesh):
    in_specs = (
        P("exp", "ctx"),
        P("ctx", "exp"),
        P("ctx", "exp"),
        P("ctx", "exp"),
        P(),
        P(),
        P("exp", "ctx"),
        P("ctx"),
        P("ctx", None),
        P("exp", None),
        P("exp", None),
        P("exp", None, "ctx"),
        P("exp", None, "ctx"),
        P("exp", None, "ctx"),
    )
    out_specs = P("exp", "ctx")
    return jax.shard_map(
        per_device, mesh=mesh, in_specs=in_specs, out_specs=out_specs, check_vma=False
    )
```

profile of v0, /device:TPU:1, one launch (start us, length us, event | category | flops | bytes accessed | tf_op | source)
XLA Modules:
  0.0 1161.9 jit_solution(5624072325766790315)
XLA Ops:
  6.5 1.0 compare_reduce_fusion
  7.6 0.8 compare_reduce_fusion.1
  8.3 0.1 copy.41
  8.4 0.1 broadcast_bitcast_fusion
  8.5 82.7 %all_gather.9 = bf16[512,768]{1,0:T(8,128)(2,1)S(1)} all-gather(bf16[8,768]{1,0:T(8,128)(2,1)} %param.15), channel_id=1, replica_groups=mesh['ctx'=64,'exp'=8] {'ctx'}, dimensions={0}, use_global_device_ids=true | all-gather | bytes 798720 | tf_op jit(solution)/shard_map/all_gather | solution.py:30
  91.3 0.3 copy.42
  91.5 0.1 broadcast_in_dim.67
  91.6 4.8 fusion
  96.4 221.4 %pmax.7 = f32[512,6]{0,1:T(8,128)S(1)} all-reduce(f32[512,6]{0,1:T(8,128)S(1)} %get-tuple-element.7), channel_id=1, replica_groups=mesh['ctx'=64,'exp'=8] {'ctx'}, use_global_device_ids=true, to_apply=%region_3.4 | all-reduce | flops 3072 | bytes 24576 | tf_op jit(solution)/shard_map/pmax | solution.py:48
  317.8 5.6 fusion.13
  323.4 0.0 reduce-scatter.2.cloned.1.call-start
  323.5 4.1 convert_reduce_fusion
  327.6 219.7 %psum.29 = f32[512,6]{0,1:T(8,128)S(1)} all-reduce(f32[512,6]{0,1:T(8,128)S(1)} %convert_reduce_fusion), channel_id=1, replica_groups=mesh['ctx'=64,'exp'=8] {'ctx'}, use_global_device_ids=true, to_apply=%region_6.7 | all-reduce | flops 3072 | bytes 24576 | tf_op jit(solution)/shard_map/psum | solution.py:52
  547.3 113.2 %all-reduce.2.cloned.1.call-done = f32[512,1,6,128]{3,0,2,1:T(8,128)} async-done(((f32[512,1,6,128]{3,0,2,1:T(8,128)}), f32[512,1,6,128]{3,0,2,1:T(8,128)}) %all-reduce.2.cloned.1.call-update) | async-done | bytes 1572880 | tf_op jit(solution)/shard_map/psum | solution.py:52
  660.5 1.9 divide_convert_fusion
  662.4 0.3 copy.45
  662.7 1.1 fusion.44
  663.8 0.0 reduce-scatter.2.cloned.1.call-update
  663.8 0.0 all-gather.3.cloned.1.call-start
  663.9 0.6 compare_and_fusion
  664.5 0.6 copy-done.6
  665.0 0.7 fusion.37
  665.7 45.5 %reduce-scatter.2.cloned.1.call-done = f32[64,96]{1,0:T(8,128)} async-done(((f32[512,96]{1,0:T(8,128)}), f32[64,96]{1,0:T(8,128)}) %reduce-scatter.2.cloned.1.call-update) | async-done | bytes 24592 | tf_op jit(solution)/shard_map/reduce_scatter | solution.py:55
  711.2 0.9 multiply_reduce_fusion.1
  712.1 115.6 %psum.30 = f32[64]{0:T(128)S(1)} all-reduce(f32[64]{0:T(128)S(1)} %multiply_reduce_fusion.1), channel_id=1, replica_groups=mesh['ctx'=64,'exp'=8] {'ctx'}, use_global_device_ids=true, to_apply=%region_9.10 | all-reduce | flops 64 | bytes 512 | tf_op jit(solution)/shard_map/psum | solution.py:64
  827.7 0.8 fusion.40
  828.5 72.3 %all-gather = bf16[64,96,64]{1,2,0:T(8,128)(2,1)S(1)} all-gather(bf16[1,96,64]{1,2,0:T(8,128)(2,1)S(1)} %fusion.40), channel_id=1, replica_groups=mesh['ctx'=64,'exp'=8] {'ctx'}, dimensions={0}, use_global_device_ids=true | all-gather | bytes 798720 | tf_op jit(solution)/shard_map/all_gather | solution.py:80
  900.8 0.7 copy.48
  901.5 2.3 reshape.108
  903.8 1.8 convolution_convert_fusion
  905.7 2.1 reshape.89
  907.8 88.6 %all_to_all.10 = bf16[8,20,6144]{2,1,0:T(8,128)(2,1)S(1)} all-to-all(bf16[8,20,6144]{2,1,0:T(8,128)(2,1)} %reshape.89), channel_id=1, replica_groups=mesh['ctx'=64,'exp'=8] {'exp'}, dimensions={0} | all-to-all | bytes 3932160 | tf_op jit(solution)/shard_map/all_to_all | solution.py:85
  996.5 0.8 fusion.16
  997.3 0.6 copy-done.1
  997.8 1.4 fusion.25
  999.3 0.1 copy.49
  999.4 0.1 reshape.99
  999.5 0.1 copy.47
  999.7 0.2 fusion.39
  999.9 113.2 %psum.31 = f32[64,8]{0,1:T(8,128)S(1)} all-reduce(f32[64,8]{0,1:T(8,128)S(1)} %fusion.39), channel_id=1, replica_groups=mesh['ctx'=64,'exp'=8] {'ctx'}, use_global_device_ids=true, to_apply=%region_10.11 | all-reduce | flops 512 | bytes 4096 | tf_op jit(solution)/shard_map/psum | solution.py:66
  1113.1 9.4 all-gather.3.cloned.1.call-done
  1122.6 3.5 fusion.28
  1126.1 22.9 %all-to-all-start.1 = ((bf16[8,20,96]{2,1,0:T(8,128)(2,1)}), bf16[8,20,96]{2,1,0:T(8,128)(2,1)S(1)}, u32[]{:S(2)}, u32[]{:S(2)}) async-start(bf16[8,20,96]{2,1,0:T(8,128)(2,1)} %fusion.28), calls=%async_computation.2 | async-start | bytes 98304 | tf_op jit(solution)/shard_map/all_to_all | solution.py:97
  1149.0 0.1 copy.46
  1149.1 4.7 all-to-all-done.1
  1153.8 0.7 gather_fusion
  1154.5 0.2 multiply_reduce_fusion
  1154.7 0.6 add_convert_fusion
  (47 shorter events, 0.2 us)
Async XLA Ops:
  6.5 989.9 %copy-start = (bf16[1,6144,128]{2,1,0:T(8,128)(2,1)S(1)}, bf16[1,6144,128]{2,1,0:T(8,128)(2,1)}, u32[]{:S(2)}) copy-start(bf16[1,6144,128]{2,1,0:T(8,128)(2,1)} %param.25) | copy-start | bytes 4718596
  6.5 654.0 %all-reduce.2.cloned.1.call-start = ((), (), s32[]{:S(2)}) async-start(), calls=%async_computation.3 | async-start | bytes 3145728 | tf_op jit(solution)/shard_map/psum | solution.py:52
  91.6 226.1 %copy-start.16 = (bf16[512,128]{1,0:T(8,128)(2,1)S(1)}, bf16[512,128]{1,0:T(8,128)(2,1)}, u32[]{:S(2)}) copy-start(bf16[512,128]{1,0:T(8,128)(2,1)} %param.17) | copy-start | bytes 393220
  323.4 387.8 %reduce-scatter.2.cloned.1.call-start = ((), (), s32[]{:S(2)}) async-start(), calls=%async_computation.4 | async-start | bytes 294912 | tf_op jit(solution)/shard_map/reduce_scatter | solution.py:55
  327.6 335.1 %copy-start.4 = (bf16[768,96]{0,1:T(8,128)(2,1)S(1)}, bf16[768,96]{0,1:T(8,128)(2,1)}, u32[]{:S(2)}) copy-start(bf16[768,96]{0,1:T(8,128)(2,1)} %param.20) | copy-start | bytes 442372
  327.6 336.3 %copy-start.8 = (s32[64,2]{0,1:T(2,128)S(1)}, s32[64,2]{0,1:T(2,128)}, u32[]{:S(2)}) copy-start(s32[64,2]{0,1:T(2,128)} %param.23) | copy-start | bytes 1540
  327.6 336.3 %copy-start.11 = (s32[64,2]{0,1:T(2,128)S(1)}, s32[64,2]{0,1:T(2,128)}, u32[]{:S(2)}) copy-start(s32[64,2]{0,1:T(2,128)} %param.24) | copy-start | bytes 1540
  327.6 383.6 %copy-start.5 = (bf16[64,96]{1,0:T(8,128)(2,1)S(1)}, bf16[64,96]{1,0:T(8,128)(2,1)}, u32[]{:S(2)}) copy-start(bf16[64,96]{1,0:T(8,128)(2,1)} %param.14) | copy-start | bytes 36868
  327.6 500.0 %copy-start.12 = (f32[96]{0:T(128)S(1)}, f32[96]{0:T(128)}, u32[]{:S(2)}) copy-start(f32[96]{0:T(128)} %param.21) | copy-start | bytes 1156
  663.8 458.7 %all-gather.3.cloned.1.call-start = ((), (), s32[]{:S(2)}) async-start(), calls=%async_computation.5 | async-start | bytes 3194880 | tf_op jit(solution)/shard_map/all_gather | solution.py:93
  664.5 0.6 copy-start.6
  827.7 73.8 %copy-start.14 = (f32[64]{0:T(128)}, f32[64]{0:T(128)S(1)}, u32[]{:S(2)}) copy-start(f32[64]{0:T(128)S(1)} %add_rsqrt_fusion) | copy-start | bytes 772
  996.4 1.4 copy-start.1
  996.4 2.8 copy-start.7
  996.4 3.1 copy-start.10
  996.4 3.2 copy-start.3
  996.4 3.2 copy-start.13
  996.5 3.2 copy-start.15
  996.5 3.2 copy-start.17
  997.8 115.3 %copy-start.9 = (s32[64,2]{0,1:T(2,128)S(1)}, s32[64,2]{0,1:T(2,128)}, u32[]{:S(2)}) copy-start(s32[64,2]{0,1:T(2,128)} %param.23) | copy-start | bytes 1540
  997.8 124.7 %copy-start.2 = (bf16[1,8192,96]{1,2,0:T(8,128)(2,1)S(1)}, bf16[1,8192,96]{1,2,0:T(8,128)(2,1)}, u32[]{:S(2)}) copy-start(bf16[1,8192,96]{1,2,0:T(8,128)(2,1)} %param.27) | copy-start | bytes 4718596
  1126.1 27.7 %all-to-all-start.1 = ((bf16[8,20,96]{2,1,0:T(8,128)(2,1)}), bf16[8,20,96]{2,1,0:T(8,128)(2,1)S(1)}, u32[]{:S(2)}, u32[]{:S(2)}) async-start(bf16[8,20,96]{2,1,0:T(8,128)(2,1)} %fusion.28), calls=%async_computation.2 | async-start | bytes 98304 | tf_op jit(solution)/shard_map/all_to_all | solution.py:97
Sparse Core Ops, SparseCore 0:
  323.6 336.9 all-reduce.1
  664.0 47.1 reduce-scatter.1
  999.4 123.1 all-gather.2
where the time goes:
time: 1160 us
  blocking collectives  914 us (79%)
  waiting for transfers between devices  173 us (15%)
  starting transfers between devices  23 us (2%)
  matrix products  19.2 us (2%)
  between operations  13.4 us (1%)
  other arithmetic  11.6 us (1%)
    pmax x1, blocking collectives, per_device(): peak = lax.pmax(local_peak, 'ctx')  221 us
    psum x1, blocking collectives, per_device(): numerator, denominator = lax.psum((numerator, denominator), 'ctx')  220 us
    psum x1, blocking collectives, per_device(): squares = lax.psum(jnp.sum(residual * residual, axis=1), 'ctx')  116 us
    psum x1, blocking collectives, per_device(): lax.psum(jnp.dot(scaled * inverse[:, None], router_wide, precision=lax.Pr...  113 us
    psum x1, waiting for transfers between devices, per_device(): numerator, denominator = lax.psum((numerator, denominator), 'ctx')  113 us
    all_to_all x1, blocking collectives, per_device(): lax.all_to_all(outgoing, 'exp', split_axis=0, concat_axis=0, tiled=True)  88.6 us
    all_gather x1, blocking collectives, per_device(): all_queries = lax.all_gather(queries, 'ctx', axis=0, tiled=True)  82.7 us
    all_gather x1, blocking collectives, per_device(): feature_rows = lax.all_gather(normed, 'ctx', axis=1, tiled=True)  72.3 us
  transfers between devices with their start and end apart: 4, of which 4 were waited for; matrix products, arithmetic and copies ran while one was open for 1% of the time, Pallas kernels for 0%

commit v1 on v0

--- a/solution.py
+++ b/solution.py
@@ -63,9 +63,8 @@
     router_wide = router.astype(jnp.float32)
     squares = lax.psum(jnp.sum(residual * residual, axis=1), "ctx")
     inverse = lax.rsqrt(squares / D + eps)
-    logits = lax.psum(
-        jnp.dot(scaled * inverse[:, None], router_wide, precision=lax.Precision.HIGHEST), "ctx"
-    )
+    body = jnp.dot(scaled * inverse[:, None], router_wide, precision=lax.Precision.HIGHEST)
+    logits = lax.all_gather(body, axis_name="ctx").sum(axis=0)
     normed = (scaled * inverse[:, None]).astype(jnp.bfloat16)
     experts_all = router.shape[1]
     onehot = expert_ids[:, :, None] == jnp.arange(experts_all, dtype=jnp.int32)[None, None, :]

time: 1160 us -> 1150 us (level)
  blocking collectives: 914 us -> 866 us
  waiting for transfers between devices: 173 us -> 220 us
    psum x1 -> x0, blocking collectives: 113 us -> none  [per_device(): lax.psum(jnp.dot(scaled * inverse[:, None], router_wide, precision=lax.Pr...]
    all_gather x0 -> x1, blocking collectives: none -> 65.6 us  [per_device(): logits = lax.all_gather(body, axis_name='ctx').sum(axis=0)]
    all_gather x1, waiting for transfers between devices: 9.44 us -> 56.9 us  [per_device(): lax.all_gather(hidden, 'ctx', axis=3, tiled=True)]
where the time goes in v1:
time: 1150 us
  blocking collectives  866 us (75%)
  waiting for transfers between devices  220 us (19%)
  matrix products  19.2 us (2%)
  starting transfers between devices  14.1 us (1%)
  between operations  13.4 us (1%)
  other arithmetic  11.7 us (1%)
    pmax x1, blocking collectives, per_device(): peak = lax.pmax(local_peak, 'ctx')  221 us
    psum x1, blocking collectives, per_device(): numerator, denominator = lax.psum((numerator, denominator), 'ctx')  220 us
    psum x1, blocking collectives, per_device(): squares = lax.psum(jnp.sum(residual * residual, axis=1), 'ctx')  116 us
    psum x1, waiting for transfers between devices, per_device(): numerator, denominator = lax.psum((numerator, denominator), 'ctx')  113 us
    all_to_all x1, blocking collectives, per_device(): lax.all_to_all(outgoing, 'exp', split_axis=0, concat_axis=0, tiled=True)  88.6 us
    all_gather x1, blocking collectives, per_device(): all_queries = lax.all_gather(queries, 'ctx', axis=0, tiled=True)  82.7 us
    all_gather x1, blocking collectives, per_device(): feature_rows = lax.all_gather(normed, 'ctx', axis=1, tiled=True)  72.3 us
    all_gather x1, blocking collectives, per_device(): logits = lax.all_gather(body, axis_name='ctx').sum(axis=0)  65.6 us
  transfers between devices with their start and end apart: 4, of which 4 were waited for; matrix products, arithmetic and copies ran while one was open for 1% of the time, Pallas kernels for 0%

profile of v1, /device:TPU:1, one launch (start us, length us, event | category | flops | bytes accessed | tf_op | source)
XLA Modules:
  0.0 1152.7 jit_solution(11805528375181506239)
XLA Ops:
  6.5 1.0 compare_reduce_fusion
  7.6 0.8 compare_reduce_fusion.1
  8.3 0.1 copy.39
  8.4 0.1 broadcast_bitcast_fusion
  8.5 82.7 %all_gather.15 = bf16[512,768]{1,0:T(8,128)(2,1)S(1)} all-gather(bf16[8,768]{1,0:T(8,128)(2,1)} %param.15), channel_id=1, replica_groups=mesh['ctx'=64,'exp'=8] {'ctx'}, dimensions={0}, use_global_device_ids=true | all-gather | bytes 798720 | tf_op jit(solution)/shard_map/all_gather | solution.py:30
  91.3 0.3 copy.40
  91.5 0.1 broadcast_in_dim.67
  91.6 4.8 fusion
  96.4 221.4 %pmax.7 = f32[512,6]{0,1:T(8,128)S(1)} all-reduce(f32[512,6]{0,1:T(8,128)S(1)} %get-tuple-element.7), channel_id=1, replica_groups=mesh['ctx'=64,'exp'=8] {'ctx'}, use_global_device_ids=true, to_apply=%region_3.4 | all-reduce | flops 3072 | bytes 24576 | tf_op jit(solution)/shard_map/pmax | solution.py:48
  317.8 5.6 fusion.13
  323.4 0.0 reduce-scatter.2.cloned.1.call-start
  323.5 4.1 convert_reduce_fusion
  327.6 219.7 %psum.22 = f32[512,6]{0,1:T(8,128)S(1)} all-reduce(f32[512,6]{0,1:T(8,128)S(1)} %convert_reduce_fusion), channel_id=1, replica_groups=mesh['ctx'=64,'exp'=8] {'ctx'}, use_global_device_ids=true, to_apply=%region_6.7 | all-reduce | flops 3072 | bytes 24576 | tf_op jit(solution)/shard_map/psum | solution.py:52
  547.3 113.2 %all-reduce.2.cloned.1.call-done = f32[512,1,6,128]{3,0,2,1:T(8,128)} async-done(((f32[512,1,6,128]{3,0,2,1:T(8,128)}), f32[512,1,6,128]{3,0,2,1:T(8,128)}) %all-reduce.2.cloned.1.call-update) | async-done | bytes 1572880 | tf_op jit(solution)/shard_map/psum | solution.py:52
  660.5 1.9 divide_convert_fusion
  662.4 0.3 copy.43
  662.7 1.1 fusion.43
  663.8 0.0 all-gather.5.cloned.1.call-start
  663.9 0.6 compare_and_fusion
  664.5 0.6 copy-done.6
  665.0 0.7 fusion.37
  665.7 45.5 %reduce-scatter.2.cloned.1.call-done = f32[64,96]{1,0:T(8,128)} async-done(((f32[512,96]{1,0:T(8,128)}), f32[64,96]{1,0:T(8,128)}) %reduce-scatter.2.cloned.1.call-update) | async-done | bytes 24592 | tf_op jit(solution)/shard_map/reduce_scatter | solution.py:55
  711.2 0.9 multiply_reduce_fusion.1
  712.1 115.6 %psum.23 = f32[64]{0:T(128)S(1)} all-reduce(f32[64]{0:T(128)S(1)} %multiply_reduce_fusion.1), channel_id=1, replica_groups=mesh['ctx'=64,'exp'=8] {'ctx'}, use_global_device_ids=true, to_apply=%region_9.10 | all-reduce | flops 64 | bytes 512 | tf_op jit(solution)/shard_map/psum | solution.py:64
  827.7 0.8 fusion.39
  828.5 72.3 %all-gather.2 = bf16[64,96,64]{1,2,0:T(8,128)(2,1)S(1)} all-gather(bf16[1,96,64]{1,2,0:T(8,128)(2,1)S(1)} %fusion.39), channel_id=1, replica_groups=mesh['ctx'=64,'exp'=8] {'ctx'}, dimensions={0}, use_global_device_ids=true | all-gather | bytes 798720 | tf_op jit(solution)/shard_map/all_gather | solution.py:79
  900.8 0.7 copy.46
  901.5 2.3 reshape.111
  903.8 1.8 convolution_convert_fusion
  905.7 2.1 reshape.89
  907.8 88.6 %all_to_all.10 = bf16[8,20,6144]{2,1,0:T(8,128)(2,1)S(1)} all-to-all(bf16[8,20,6144]{2,1,0:T(8,128)(2,1)} %reshape.89), channel_id=1, replica_groups=mesh['ctx'=64,'exp'=8] {'exp'}, dimensions={0} | all-to-all | bytes 3932160 | tf_op jit(solution)/shard_map/all_to_all | solution.py:84
  996.5 0.8 fusion.16
  997.3 0.6 copy-done.1
  997.8 1.4 fusion.25
  999.3 0.1 copy.47
  999.4 0.1 reshape.99
  999.5 0.1 copy.45
  999.7 0.2 convolution_bitcast_fusion
  999.9 65.6 %all-gather.1 = f32[64,64,8]{1,2,0:T(8,128)S(1)} all-gather(f32[1,64,8]{1,2,0:T(8,128)S(1)} %convolution_bitcast_fusion), channel_id=2, replica_groups=mesh['ctx'=64,'exp'=8] {'ctx'}, dimensions={0}, use_global_device_ids=true | all-gather | bytes 133120 | tf_op jit(solution)/shard_map/all_gather | solution.py:67
  1065.4 0.1 reduce_sum.62
  1065.5 56.9 %all-gather.5.cloned.1.call-done = bf16[8,1,20,8192]{3,2,0,1:T(8,128)(2,1)} async-done(((bf16[8,1,20,128]{3,2,0,1:T(8,128)(2,1)}), bf16[8,1,20,8192]{3,2,0,1:T(8,128)(2,1)}) %all-gather.5.cloned.1.call-update) | async-done | bytes 2621456 | tf_op jit(solution)/shard_map/all_gather | solution.py:92
  1122.4 3.5 fusion.28
  1125.9 14.0 %all-to-all-start.1 = ((bf16[8,20,96]{2,1,0:T(8,128)(2,1)}), bf16[8,20,96]{2,1,0:T(8,128)(2,1)S(1)}, u32[]{:S(2)}, u32[]{:S(2)}) async-start(bf16[8,20,96]{2,1,0:T(8,128)(2,1)} %fusion.28), calls=%async_computation.2 | async-start | bytes 98304 | tf_op jit(solution)/shard_map/all_to_all | solution.py:96
  1139.9 0.1 copy.44
  1140.0 4.7 all-to-all-done.1
  1144.7 0.7 gather_fusion
  1145.4 0.2 multiply_reduce_fusion
  1145.6 0.6 add_convert_fusion
  (48 shorter events, 0.3 us)
Async XLA Ops:
  6.5 989.9 %copy-start = (bf16[1,6144,128]{2,1,0:T(8,128)(2,1)S(1)}, bf16[1,6144,128]{2,1,0:T(8,128)(2,1)}, u32[]{:S(2)}) copy-start(bf16[1,6144,128]{2,1,0:T(8,128)(2,1)} %param.25) | copy-start | bytes 4718596
  6.5 654.0 %all-reduce.2.cloned.1.call-start = ((), (), s32[]{:S(2)}) async-start(), calls=%async_computation.3 | async-start | bytes 3145728 | tf_op jit(solution)/shard_map/psum | solution.py:52
  91.6 226.1 %copy-start.16 = (bf16[512,128]{1,0:T(8,128)(2,1)S(1)}, bf16[512,128]{1,0:T(8,128)(2,1)}, u32[]{:S(2)}) copy-start(bf16[512,128]{1,0:T(8,128)(2,1)} %param.17) | copy-start | bytes 393220
  323.4 387.8 %reduce-scatter.2.cloned.1.call-start = ((), (), s32[]{:S(2)}) async-start(), calls=%async_computation.4 | async-start | bytes 294912 | tf_op jit(solution)/shard_map/reduce_scatter | solution.py:55
  327.6 335.1 %copy-start.4 = (bf16[768,96]{0,1:T(8,128)(2,1)S(1)}, bf16[768,96]{0,1:T(8,128)(2,1)}, u32[]{:S(2)}) copy-start(bf16[768,96]{0,1:T(8,128)(2,1)} %param.20) | copy-start | bytes 442372
  327.6 336.3 %copy-start.8 = (s32[64,2]{0,1:T(2,128)S(1)}, s32[64,2]{0,1:T(2,128)}, u32[]{:S(2)}) copy-start(s32[64,2]{0,1:T(2,128)} %param.23) | copy-start | bytes 1540
  327.6 336.3 %copy-start.11 = (s32[64,2]{0,1:T(2,128)S(1)}, s32[64,2]{0,1:T(2,128)}, u32[]{:S(2)}) copy-start(s32[64,2]{0,1:T(2,128)} %param.24) | copy-start | bytes 1540
  327.6 383.6 %copy-start.5 = (bf16[64,96]{1,0:T(8,128)(2,1)S(1)}, bf16[64,96]{1,0:T(8,128)(2,1)}, u32[]{:S(2)}) copy-start(bf16[64,96]{1,0:T(8,128)(2,1)} %param.14) | copy-start | bytes 36868
  327.6 500.0 %copy-start.12 = (f32[96]{0:T(128)S(1)}, f32[96]{0:T(128)}, u32[]{:S(2)}) copy-start(f32[96]{0:T(128)} %param.21) | copy-start | bytes 1156
  663.8 458.6 %all-gather.5.cloned.1.call-start = ((), (), s32[]{:S(2)}) async-start(), calls=%async_computation.5 | async-start | bytes 3194880 | tf_op jit(solution)/shard_map/all_gather | solution.py:92
  664.5 0.6 copy-start.6
  827.7 73.8 %copy-start.14 = (f32[64]{0:T(128)}, f32[64]{0:T(128)S(1)}, u32[]{:S(2)}) copy-start(f32[64]{0:T(128)S(1)} %add_rsqrt_fusion) | copy-start | bytes 772
  996.4 1.4 copy-start.1
  996.4 2.8 copy-start.7
  996.4 3.1 copy-start.10
  996.4 3.2 copy-start.3
  996.4 3.2 copy-start.13
  996.5 3.2 copy-start.15
  996.5 3.2 copy-start.17
  997.8 67.7 %copy-start.9 = (s32[64,2]{0,1:T(2,128)S(1)}, s32[64,2]{0,1:T(2,128)}, u32[]{:S(2)}) copy-start(s32[64,2]{0,1:T(2,128)} %param.23) | copy-start | bytes 1540
  997.8 124.6 %copy-start.2 = (bf16[1,8192,96]{1,2,0:T(8,128)(2,1)S(1)}, bf16[1,8192,96]{1,2,0:T(8,128)(2,1)}, u32[]{:S(2)}) copy-start(bf16[1,8192,96]{1,2,0:T(8,128)(2,1)} %param.27) | copy-start | bytes 4718596
  1125.9 18.8 %all-to-all-start.1 = ((bf16[8,20,96]{2,1,0:T(8,128)(2,1)}), bf16[8,20,96]{2,1,0:T(8,128)(2,1)S(1)}, u32[]{:S(2)}, u32[]{:S(2)}) async-start(bf16[8,20,96]{2,1,0:T(8,128)(2,1)} %fusion.28), calls=%async_computation.2 | async-start | bytes 98304 | tf_op jit(solution)/shard_map/all_to_all | solution.py:96
Sparse Core Ops, SparseCore 0:
  323.6 336.9 all-reduce.1
  664.0 47.1 reduce-scatter.1
  999.4 122.9 all-gather.4
